TPU v7x, 256 devices: a whole 4x4x8 slice. The times are simulated.
256 devices in a mesh: seq: 32 (over z, y), head: 8 (over x, core).
Axes of the slice: x: 4, y: 4, z: 8, core: 2. Of those that a mesh axis runs over, the one named last changes fastest.
Arguments:
- query: bfloat16 [49152, 3072], P(('seq', 'head')), may hold values from -40 to 40
- key: bfloat16 [49152, 3072], P(('seq', 'head')), may hold values from -4 to 4
- value: bfloat16 [49152, 3072], P(('seq', 'head')), may hold values from -6 to 6
- raster_to_tile: int32 [49152], P(('seq', 'head')), may hold values from 0 to 49151, as said below
- window_list: int32 [128, 4], P('seq'), may hold values from 0 to 127, as said below
- valid_count: int32 [128], replicated, may hold values from 96 to 384
Outputs:
- attended: bfloat16 [49152, 3072], P(('seq', 'head'))
Inputs may be any that keep to these rules, and one draw needn't show every extreme that they name: `raster_to_tile`: A permutation of the slots. Raster shard d (rows d * 1536 // 8 onward, d counting seq+head) holds exactly 6 slots of every owner o, where owner o holds slots o * 1536 to (o+1) * 1536 - 1. `window_list`: row t holds t first, then 4 - 1 distinct other tiles, each within 3 tiles of t.
All inputs are finite; a program needn't handle non-finite values.
Results may differ from a plain program's by a relative error of at most 0.0036.
Values may be sent and summed in bfloat16 or wider, within the bound.
A program may use at most 64 MiB of HBM per device.

v0:
```python
import jax
import jax.numpy as jnp
from jax import lax
from jax.sharding import PartitionSpec as P

HEAD_DIM = 128


def body(query, key, value, raster_to_tile, window_list, valid_count):
    seq_count = lax.axis_size("seq")
    head_count = lax.axis_size("head")
    seq_pos = lax.axis_index("seq")
    rows_here, width = query.shape
    part_width = width // head_count
    tile_dev, win = window_list.shape
    tok_dev = rows_here * head_count
    tile = tok_dev // tile_dev
    share = rows_here // seq_count
    reach = win - 1
    rim = reach * tile
    ext_rows = tok_dev + 2 * rim
    ext_tiles = tile_dev + 2 * reach
    heads_here = part_width // HEAD_DIM
    all_tiles = valid_count.shape[0]
    order = jnp.argsort(raster_to_tile)
    slots_sorted = raster_to_tile[order].reshape(seq_count, share)
    query_sorted = query[order].reshape(seq_count, share, head_count, part_width)
    joined = jnp.concatenate(
        [
            key.reshape(rows_here, head_count, part_width),
            value.reshape(rows_here, head_count, part_width),
        ],
        axis=2,
    )
    pair_sorted = joined[order].reshape(seq_count, share, head_count, 2 * part_width)
    zero_pair = jnp.zeros_like(pair_sorted[:1])
    wide_pair = jnp.concatenate(
        [
            jnp.concatenate([zero_pair, pair_sorted[:-1]], axis=0),
            pair_sorted,
            jnp.concatenate([pair_sorted[1:], zero_pair], axis=0),
        ],
        axis=1,
    )
    empty_slots = jnp.full((1, share), -1, jnp.int32)
    wide_slots = jnp.concatenate(
        [
            jnp.concatenate([empty_slots, slots_sorted[:-1]], axis=0),
            slots_sorted,
            jnp.concatenate([slots_sorted[1:], empty_slots], axis=0),
        ],
        axis=1,
    )
    slot_send = jnp.broadcast_to(wide_slots[:, :, None], (seq_count, 3 * share, head_count))
    query_in, pair_in, slot_in = (
        lax.all_to_all(
            lax.all_to_all(query_sorted, "seq", split_axis=0, concat_axis=0, tiled=True),
            "head",
            split_axis=2,
            concat_axis=1,
            tiled=True,
        ),
        lax.all_to_all(
            lax.all_to_all(wide_pair, "seq", split_axis=0, concat_axis=0, tiled=True),
            "head",
            split_axis=2,
            concat_axis=1,
            tiled=True,
        ),
        lax.all_to_all(
            lax.all_to_all(slot_send, "seq", split_axis=0, concat_axis=0, tiled=True),
            "head",
            split_axis=2,
            concat_axis=1,
            tiled=True,
        ),
    )
    middle = slot_in.reshape(seq_count, head_count, 3, share)[:, :, 1, :]
    local = middle.reshape(tok_dev) - seq_pos * tok_dev
    place = jnp.zeros((tok_dev,), jnp.int32).at[local].set(jnp.arange(tok_dev, dtype=jnp.int32))
    query_tile = query_in.reshape(tok_dev, part_width)[place]
    every_slot = slot_in.reshape(3 * tok_dev)
    shifted = every_slot - (seq_pos * tok_dev - rim)
    target = jnp.where((every_slot >= 0) & (shifted >= 0) & (shifted < ext_rows), shifted, ext_rows)
    place_ext = (
        jnp.full((ext_rows,), 3 * tok_dev, jnp.int32)
        .at[target]
        .set(jnp.arange(3 * tok_dev, dtype=jnp.int32), mode="drop")
    )
    padded = jnp.concatenate(
        [
            pair_in.reshape(3 * tok_dev, 2 * part_width),
            jnp.zeros((1, 2 * part_width), pair_in.dtype),
        ],
        axis=0,
    )
    pair_ext = padded[place_ext]
    first_tile = seq_pos * tile_dev - reach
    global_tiles = jnp.clip(first_tile + jnp.arange(ext_tiles, dtype=jnp.int32), 0, all_tiles - 1)
    key_usable = jnp.arange(tile, dtype=jnp.int32)[None, :] < valid_count[global_tiles][:, None]
    own_usable = key_usable[reach : reach + tile_dev]
    local_windows = window_list - first_tile
    query_blocks = query_tile.reshape(tile_dev, tile, heads_here, HEAD_DIM)
    pair_blocks = pair_ext.reshape(ext_tiles, tile, 2, heads_here, HEAD_DIM)
    scale = HEAD_DIM ** (-0.5)

    def one_tile(item):
        query_blk, windows, query_usable = item
        picked = pair_blocks[windows]
        keys_blk = picked[:, :, 0].reshape(win * tile, heads_here, HEAD_DIM)
        values_blk = picked[:, :, 1].reshape(win * tile, heads_here, HEAD_DIM)
        usable = key_usable[windows].reshape(win * tile)
        scores = (
            jnp.einsum("qhd,khd->hqk", query_blk, keys_blk, preferred_element_type=jnp.float32)
            * scale
        )
        scores = jnp.where(usable[None, None, :], scores, -jnp.inf)
        top = jnp.max(scores, axis=2, keepdims=True)
        weights = jnp.exp(scores - top)
        total = jnp.sum(weights, axis=2)
        mixed = jnp.einsum(
            "hqk,khd->qhd",
            weights.astype(jnp.bfloat16),
            values_blk,
            preferred_element_type=jnp.float32,
        )
        mixed = mixed / jnp.transpose(total)[:, :, None]
        mixed = jnp.where(query_usable[:, None, None], mixed, 0.0)
        return mixed.astype(jnp.bfloat16).reshape(tile, part_width)

    out_tile = lax.map(one_tile, (query_blocks, local_windows, own_usable)).reshape(
        tok_dev, part_width
    )
    outgoing = out_tile[local].reshape(seq_count, head_count, share, 1, part_width)
    arrived = lax.all_to_all(
        lax.all_to_all(outgoing, "seq", split_axis=0, concat_axis=0, tiled=True),
        "head",
        split_axis=1,
        concat_axis=3,
        tiled=True,
    )
    sorted_rows = arrived.reshape(rows_here, width)
    inverse = (
        jnp.zeros((rows_here,), jnp.int32).at[order].set(jnp.arange(rows_here, dtype=jnp.int32))
    )
    return sorted_rows[inverse]


def solution(mesh):
    placed = (
        P(("seq", "head"), None),
        P(("seq", "head"), None),
        P(("seq", "head"), None),
        P(("seq", "head")),
        P("seq", None),
        P(),
    )
    return jax.shard_map(
        body, mesh=mesh, in_specs=placed, out_specs=P(("seq", "head"), None), check_vma=False
    )
```

profile of v0, /device:TPU:1, one launch (start us, length us, event | category | flops | bytes accessed | tf_op | source)
XLA Modules:
  0.0 554.6 jit_solution(8304889225877488797)
XLA Ops:
  0.0 3.9 sort.17
  6.6 20.5 %all_to_all.80 = s32[32,1,144]{2,1,0:T(1,128)S(1)} all-to-all(s32[32,1,144]{2,1,0:T(1,128)S(1)} %reshape.329), channel_id=1, replica_groups=mesh['seq'=32,'head'=8] {'seq'}, dimensions={0} | all-to-all | bytes 36864 | tf_op jit(solution)/shard_map/all_to_all | solution.py:71
  29.4 6.4 %all-to-all-start.3 = ((s32[8,1,576]{2,1,0:T(1,128)}), s32[8,1,576]{2,1,0:T(1,128)}, u32[]{:S(2)}, u32[]{:S(2)}) async-start(s32[8,1,576]{2,1,0:T(1,128)} %reshape.331), calls=%async_computation.3 | async-start | bytes 40960 | tf_op jit(solution)/shard_map/all_to_all | solution.py:70
  40.6 4.1 all-to-all-start.4
  49.6 3.3 fusion.37
  52.9 21.1 %all-to-all-done.4 = bf16[32,6,8,384]{3,2,1,0:T(8,128)(2,1)S(1)} async-done(((bf16[32,6,8,384]{3,2,1,0:T(8,128)(2,1)}), bf16[32,6,8,384]{3,2,1,0:T(8,128)(2,1)S(1)}, u32[]{:S(2)}, u32[]{:S(2)}) %all-to-all-start.4) | async-done | bytes 1179680 | tf_op jit(solution)/shard_map/all_to_all | solution.py:57
  74.0 6.5 %all-to-all-start = ((bf16[32,18,8,768]{3,2,1,0:T(8,128)(2,1)}), bf16[32,18,8,768]{3,2,1,0:T(8,128)(2,1)}, u32[]{:S(2)}, u32[]{:S(2)}) async-start(bf16[32,18,8,768]{3,2,1,0:T(8,128)(2,1)} %fusion.37), calls=%async_computation | async-start | bytes 14155776 | tf_op jit(solution)/shard_map/all_to_all | solution.py:64
  81.8 152.8 %all-to-all-done = bf16[32,18,8,768]{3,2,1,0:T(8,128)(2,1)} async-done(((bf16[32,18,8,768]{3,2,1,0:T(8,128)(2,1)}), bf16[32,18,8,768]{3,2,1,0:T(8,128)(2,1)}, u32[]{:S(2)}, u32[]{:S(2)}) %all-to-all-start) | async-done | bytes 7077920 | tf_op jit(solution)/shard_map/all_to_all | solution.py:64
  234.5 9.1 %all-to-all-start.5 = ((bf16[32,6,8,384]{3,0,1,2:T(8,128)(2,1)}), bf16[32,6,8,384]{3,0,1,2:T(8,128)(2,1)S(1)}, u32[]{:S(2)}, u32[]{:S(2)}) async-start(bf16[32,6,8,384]{3,0,1,2:T(8,128)(2,1)} %copy.50), calls=%async_computation.5 | async-start | bytes 2359296 | tf_op jit(solution)/shard_map/all_to_all | solution.py:56
  243.7 8.3 %copy.44 = bf16[32,18,8,768]{3,0,1,2:T(8,128)(2,1)} copy(bf16[32,18,8,768]{3,2,1,0:T(8,128)(2,1)} %all-to-all-done) | data formatting | bytes 14155776 | tf_op jit(solution)/shard_map/all_to_all | solution.py:64
  252.0 8.2 %all-to-all-done.5 = bf16[32,6,8,384]{3,0,1,2:T(8,128)(2,1)S(1)} async-done(((bf16[32,6,8,384]{3,0,1,2:T(8,128)(2,1)}), bf16[32,6,8,384]{3,0,1,2:T(8,128)(2,1)S(1)}, u32[]{:S(2)}, u32[]{:S(2)}) %all-to-all-start.5) | async-done | bytes 1179680 | tf_op jit(solution)/shard_map/all_to_all | solution.py:56
  260.2 5.6 %all-to-all-start.1 = ((bf16[32,18,8,768]{3,0,1,2:T(8,128)(2,1)}), bf16[32,18,8,768]{3,0,1,2:T(8,128)(2,1)}, u32[]{:S(2)}, u32[]{:S(2)}) async-start(bf16[32,18,8,768]{3,0,1,2:T(8,128)(2,1)} %copy.44), calls=%async_computation.1 | async-start | bytes 14155776 | tf_op jit(solution)/shard_map/all_to_all | solution.py:63
  269.2 6.2 %scatter_custom_fusion.1 = s32[1536]{0:T(1024)S(1)} fusion(s32[1536]{0:T(1024)S(1)} %fusion.42, s32[1536]{0:T(1024)S(1)} %iota.24, s32[]{:T(128)} %constant.29.clone.1), kind=kCustom, calls=%fused_computation.70 | custom fusion | bytes 6148 | tf_op jit(solution)/shard_map/scatter | solution.py:80
  275.5 17.6 %scatter_custom_fusion = s32[3840]{0:T(1024)S(1)} fusion(s32[4608]{0:T(1024)S(1)} %fusion.39, s32[4608]{0:T(1024)S(1)} %iota.23, s32[]{:T(128)} %constant.14.clone.1), kind=kCustom, calls=%fused_computation.63 | custom fusion | bytes 15364 | tf_op jit(solution)/shard_map/scatter | solution.py:88
  297.1 5.3 gather_fusion.7
  302.4 3.3 reshape.319
  307.0 38.6 %all-to-all-done.1 = bf16[32,18,8,768]{3,0,1,2:T(8,128)(2,1)} async-done(((bf16[32,18,8,768]{3,0,1,2:T(8,128)(2,1)}), bf16[32,18,8,768]{3,0,1,2:T(8,128)(2,1)}, u32[]{:S(2)}, u32[]{:S(2)}) %all-to-all-start.1) | async-done | bytes 7077920 | tf_op jit(solution)/shard_map/all_to_all | solution.py:63
  345.6 10.9 %copy.45 = bf16[32,8,18,1,768]{4,2,1,0,3:T(8,128)(2,1)} copy(bf16[32,8,18,1,768]{4,0,2,1,3:T(8,128)(2,1)} %bitcast.5) | data formatting | bytes 14155776 | tf_op jit(solution)/shard_map/all_to_all | solution.py:63
  356.5 11.5 %reshape.193 = bf16[4608,768]{1,0:T(8,128)(2,1)} reshape(bf16[32,8,18,1,768]{4,2,1,0,3:T(8,128)(2,1)} %copy.45) | data formatting | bytes 14155776 | tf_op jit(solution)/shard_map/reshape | solution.py:92
  368.0 6.4 %concatenate.28 = bf16[4609,768]{1,0:T(8,128)(2,1)} pad(bf16[4608,768]{1,0:T(8,128)(2,1)} %reshape.193, bf16[]{:T(256)} %constant.30.clone.1), padding=0_1x0_0 | pad | bytes 14157314 | tf_op jit(solution)/shard_map/concatenate | solution.py:90
  374.3 18.8 %gather_fusion.5 = bf16[3840,768]{1,0:T(8,128)(2,1)} fusion(bf16[4609,768]{1,0:T(8,128)(2,1)} %concatenate.28, s32[4096]{0:T(1024)S(1)} %pad_clamp_fusion.1), kind=kCustom, calls=%fused_computation.5 | custom fusion | bytes 11811840 | tf_op jit(solution)/shard_map/gather | solution.py:97
  393.1 13.8 %reshape.195 = bf16[10,384,2,3,128]{4,3,2,1,0:T(4,128)(2,1)} reshape(bf16[3840,768]{1,0:T(8,128)(2,1)} %gather_fusion.5) | data formatting | bytes 11796480 | tf_op jit(solution)/shard_map/reshape | solution.py:104
  406.9 71.9 %while.11 = (s32[]{:T(128)}, bf16[4,384,384]{2,1,0:T(8,128)(2,1)S(1)}, pred[4,384]{1,0:T(4,128)(4,1)S(1)}, s32[4,4]{1,0:T(4,128)S(1)}, bf16[10,384,2,3,128]{4,3,...) while((s32[]{:T(128)}, ...), condition=%wide.region_6.7_spmd.clone, body=%wide.region_3.6_spmd.clone.sunk | while | flops 925878784 | bytes 37202520 | solution.py:131
  407.6 8.1 %gather_fusion.1 = bf16[4,384,2,3,128]{4,3,2,1,0:T(4,128)(2,1)} fusion(bf16[10,384,2,3,128]{4,3,2,1,0:T(4,128)(2,1)} %get-tuple-element.185, s32[1024]{0:T(1024)S(1)} %pad_clamp_fusion.8), kind=kCustom, calls=%fused_computation.clone.clone.1 | custom fusion | bytes 4718608 | tf_op jit(solution)/shard_map/while/body/eval_jaxpr/gather | solution.py:109
  415.6 3.0 fusion.64
  425.6 8.1 %gather_fusion.1 = bf16[4,384,2,3,128]{4,3,2,1,0:T(4,128)(2,1)} fusion(bf16[10,384,2,3,128]{4,3,2,1,0:T(4,128)(2,1)} %get-tuple-element.185, s32[1024]{0:T(1024)S(1)} %pad_clamp_fusion.8), kind=kCustom, calls=%fused_computation.clone.clone.1 | custom fusion | bytes 4718608 | tf_op jit(solution)/shard_map/while/body/eval_jaxpr/gather | solution.py:109
  443.6 8.1 %gather_fusion.1 = bf16[4,384,2,3,128]{4,3,2,1,0:T(4,128)(2,1)} fusion(bf16[10,384,2,3,128]{4,3,2,1,0:T(4,128)(2,1)} %get-tuple-element.185, s32[1024]{0:T(1024)S(1)} %pad_clamp_fusion.8), kind=kCustom, calls=%fused_computation.clone.clone.1 | custom fusion | bytes 4718608 | tf_op jit(solution)/shard_map/while/body/eval_jaxpr/gather | solution.py:109
  461.5 8.1 %gather_fusion.1 = bf16[4,384,2,3,128]{4,3,2,1,0:T(4,128)(2,1)} fusion(bf16[10,384,2,3,128]{4,3,2,1,0:T(4,128)(2,1)} %get-tuple-element.185, s32[1024]{0:T(1024)S(1)} %pad_clamp_fusion.8), kind=kCustom, calls=%fused_computation.clone.clone.1 | custom fusion | bytes 4718608 | tf_op jit(solution)/shard_map/while/body/eval_jaxpr/gather | solution.py:109
  478.8 5.3 gather_fusion.8
  486.6 40.7 %all_to_all.81 = bf16[32,8,6,1,384]{4,1,3,2,0:T(8,128)(2,1)S(1)} all-to-all(bf16[32,8,6,1,384]{4,1,3,2,0:T(8,128)(2,1)S(1)} %copy.56), channel_id=1, replica_groups=mesh['seq'=32,'head'=8] {'seq'}, dimensions={0} | all-to-all | bytes 2359296 | tf_op jit(solution)/shard_map/all_to_all | solution.py:136
  528.6 6.3 %all-to-all-start.7 = ((bf16[32,8,6,1,384]{4,0,3,2,1:T(8,128)(2,1)}), bf16[32,8,6,1,384]{4,0,3,2,1:T(8,128)(2,1)S(1)}, u32[]{:S(2)}, u32[]{:S(2)}) async-start(bf16[32,8,6,1,384]{4,0,3,2,1:T(8,128)(2,1)} %copy.57), calls=%async_computation.7 | async-start | bytes 2359296 | tf_op jit(solution)/shard_map/all_to_all | solution.py:135
  536.1 15.3 %all-to-all-done.7 = bf16[32,8,6,1,384]{4,0,3,2,1:T(8,128)(2,1)S(1)} async-done(((bf16[32,8,6,1,384]{4,0,3,2,1:T(8,128)(2,1)}), bf16[32,8,6,1,384]{4,0,3,2,1:T(8,128)(2,1)S(1)}, u32[]{:S(2)}, u32[]{:S(2)}) %all-to-all-start.7) | async-done | bytes 1179680 | tf_op jit(solution)/shard_map/all_to_all | solution.py:135
  (128 shorter events, 69.1 us)
Async XLA Ops:
  0.0 35.8 %copy-start = (bf16[192,3072]{1,0:T(8,128)(2,1)S(1)}, bf16[192,3072]{1,0:T(8,128)(2,1)}, u32[]{:S(2)}) copy-start(bf16[192,3072]{1,0:T(8,128)(2,1)} %param.8) | copy-start | bytes 3538948
  29.4 11.2 %all-to-all-start.3 = ((s32[8,1,576]{2,1,0:T(1,128)}), s32[8,1,576]{2,1,0:T(1,128)}, u32[]{:S(2)}, u32[]{:S(2)}) async-start(s32[8,1,576]{2,1,0:T(1,128)} %reshape.331), calls=%async_computation.3 | async-start | bytes 40960 | tf_op jit(solution)/shard_map/all_to_all | solution.py:70
  37.1 7.6 %copy-start.3 = (bf16[192,3072]{1,0:T(8,128)(2,1)S(1)}, bf16[192,3072]{1,0:T(8,128)(2,1)}, u32[]{:S(2)}) copy-start(bf16[192,3072]{1,0:T(8,128)(2,1)} %param.9) | copy-start | bytes 3538948
  40.6 4.3 copy-start.4
  40.6 33.4 %all-to-all-start.4 = ((bf16[32,6,8,384]{3,2,1,0:T(8,128)(2,1)}), bf16[32,6,8,384]{3,2,1,0:T(8,128)(2,1)S(1)}, u32[]{:S(2)}, u32[]{:S(2)}) async-start(bf16[32,6,8,384]{3,2,1,0:T(8,128)(2,1)} %bitcast.38), calls=%async_computation.4 | async-start | bytes 2359296 | tf_op jit(solution)/shard_map/all_to_all | solution.py:57
  74.0 160.5 %all-to-all-start = ((bf16[32,18,8,768]{3,2,1,0:T(8,128)(2,1)}), bf16[32,18,8,768]{3,2,1,0:T(8,128)(2,1)}, u32[]{:S(2)}, u32[]{:S(2)}) async-start(bf16[32,18,8,768]{3,2,1,0:T(8,128)(2,1)} %fusion.37), calls=%async_computation | async-start | bytes 14155776 | tf_op jit(solution)/shard_map/all_to_all | solution.py:64
  234.5 25.7 %all-to-all-start.5 = ((bf16[32,6,8,384]{3,0,1,2:T(8,128)(2,1)}), bf16[32,6,8,384]{3,0,1,2:T(8,128)(2,1)S(1)}, u32[]{:S(2)}, u32[]{:S(2)}) async-start(bf16[32,6,8,384]{3,0,1,2:T(8,128)(2,1)} %copy.50), calls=%async_computation.5 | async-start | bytes 2359296 | tf_op jit(solution)/shard_map/all_to_all | solution.py:56
  252.0 13.8 %copy-start.2 = (s32[128]{0:T(128)S(1)}, s32[128]{0:T(128)}, u32[]{:S(2)}) copy-start(s32[128]{0:T(128)} %param.13) | copy-start | bytes 1540
  252.0 14.6 %copy-start.5 = (s32[4,4]{1,0:T(4,128)S(1)}, s32[4,4]{1,0:T(4,128)}, u32[]{:S(2)}) copy-start(s32[4,4]{1,0:T(4,128)} %param.12) | copy-start | bytes 196
  260.2 85.4 %all-to-all-start.1 = ((bf16[32,18,8,768]{3,0,1,2:T(8,128)(2,1)}), bf16[32,18,8,768]{3,0,1,2:T(8,128)(2,1)}, u32[]{:S(2)}, u32[]{:S(2)}) async-start(bf16[32,18,8,768]{3,0,1,2:T(8,128)(2,1)} %copy.44), calls=%async_computation.1 | async-start | bytes 14155776 | tf_op jit(solution)/shard_map/all_to_all | solution.py:63
  528.6 22.8 %all-to-all-start.7 = ((bf16[32,8,6,1,384]{4,0,3,2,1:T(8,128)(2,1)}), bf16[32,8,6,1,384]{4,0,3,2,1:T(8,128)(2,1)S(1)}, u32[]{:S(2)}, u32[]{:S(2)}) async-start(bf16[32,8,6,1,384]{4,0,3,2,1:T(8,128)(2,1)} %copy.57), calls=%async_computation.7 | async-start | bytes 2359296 | tf_op jit(solution)/shard_map/all_to_all | solution.py:135
  552.3 2.3 copy-start.1
where the time goes:
time: 557 us; the launch traced here: 555 us
  waiting for transfers between devices  238 us (43%)
  local copies, waits for them, and re-layouts  182 us (33%)
  blocking collectives  61.3 us (11%)
  starting transfers between devices  37.9 us (7%)
  other arithmetic  17.9 us (3%)
  matrix products  16.8 us (3%)
    all_to_all x1, waiting for transfers between devices, body(): lax.all_to_all(wide_pair, 'seq', split_axis=0, concat_axis=0, tiled=True)  153 us
    all_to_all x1, blocking collectives, body(): lax.all_to_all(outgoing, 'seq', split_axis=0, concat_axis=0, tiled=True)  40.7 us
    all_to_all x1, waiting for transfers between devices, body(): lax.all_to_all(lax.all_to_all(wide_pair, 'seq', split_axis=0, concat_axis...  38.6 us
    gather x4, local copies, waits for them, and re-layouts, one_tile(): picked = pair_blocks[windows]  32.2 us
    all_to_all x1, waiting for transfers between devices, body(): lax.all_to_all(query_sorted, 'seq', split_axis=0, concat_axis=0, tiled=True)  21.1 us
    all_to_all x1, blocking collectives, body(): lax.all_to_all(slot_send, 'seq', split_axis=0, concat_axis=0, tiled=True)  20.5 us
    gather x1, local copies, waits for them, and re-layouts, body(): pair_ext = padded[place_ext]  18.8 us
    scatter x1, local copies, waits for them, and re-layouts, body(): place_ext = jnp.full((ext_rows,), 3 * tok_dev, jnp.int32).at[target].set(...  17.6 us
  transfers between devices with their start and end apart: 6, of which 6 were waited for; matrix products, arithmetic and copies ran while one was open for 11% of the time, Pallas kernels for 0%

commit v1 on v0

v1 whole, which is shorter than its diff:
```python
import functools

import jax
import jax.numpy as jnp
from jax import lax
from jax.experimental import pallas as pl
from jax.experimental.pallas import tpu as pltpu
from jax.sharding import PartitionSpec as P

MESH = pl.DeviceIdType.MESH
HEAD_DIM = 128
HEADS_HERE = 3
TILE = 384
WIN = 4
REACH = 3
TILE_DEV = 4
TOK_DEV = TILE * TILE_DEV
ROWS = 192
LAYERS = 8
OWNERS = 32
SHARE = TOK_DEV // OWNERS
EXT_TILES = TILE_DEV + 2 * REACH
LOG2E = 1.4426950408889634
FAR = -1e30
ORDER = (4, 3, 5, 2, 6, 1, 7)


def place(owner):
    chip, core = lax.div(owner, 2), lax.rem(owner, 2)
    x, step = lax.div(chip, 4), lax.rem(chip, 4)
    return x, step + lax.rem(x, 2) * (3 - 2 * step), core


def device(z, x, y, core):
    return (z * 4 + y, x * 2 + core)


def iota(shape, axis):
    return lax.broadcasted_iota(jnp.int32, shape, axis)


def bulk_wait(ref, sem):
    pltpu.make_async_copy(ref, ref, sem).wait()


def kernel(
    valid_ref, q_ref, k_ref, v_ref, meta_ref, out_ref,
    zkv, zq, zmeta, skv, sq, akv, aq, ekv0, ekv1, ekv2, tq, ot, oa, ox, orr,
    smeta, ameta, awin, win_smem, pos_col, slot_col, pos_row, slot_row,
    p1, p1t, p2, p2t,
    zkv_ss, zkv_rs, zq_ss, zq_rs, zm_ss, zm_rs,
    pkv_ss, pkv_rs, pq_ss, pq_rs, pm_ss, pm_rs,
    h_ss, hl_rs, hr_rs, po_ss, po_rs, zo_ss, zo_rs, win_s, pw_ss, pw_rs,
):
    ekv = (ekv0, ekv1, ekv2)
    seq, head = lax.axis_index("seq"), lax.axis_index("head")
    z, y = lax.div(seq, 4), lax.rem(seq, 4)
    x, core = lax.div(head, 2), lax.rem(head, 2)
    me = 2 * (4 * x + y + lax.rem(x, 2) * (3 - 2 * y)) + core

    def layer(j):
        return lax.rem(z + j, LAYERS)

    def peer(j):
        return lax.rem(me + j, OWNERS)

    def at_layer(zz):
        return device(zz, x, y, core)

    def at_owner(o):
        px, py, pc = place(o)
        return device(z, px, py, pc)

    barrier = pltpu.get_barrier_semaphore()

    @pl.loop(1, LAYERS)
    def _(j):
        pl.semaphore_signal(barrier, inc=1, device_id=at_layer(layer(j)), device_id_type=MESH)

    @pl.loop(1, OWNERS)
    def _(j):
        pl.semaphore_signal(barrier, inc=1, device_id=at_owner(peer(j)), device_id_type=MESH)

    pl.semaphore_wait(barrier, LAYERS - 1 + OWNERS - 1)

    def remote(src, dst, ss, rs, dev):
        pltpu.make_async_remote_copy(
            src_ref=src, dst_ref=dst, send_sem=ss, recv_sem=rs, device_id=dev, device_id_type=MESH
        ).start()

    my_rows = pl.ds(pl.multiple_of(z * ROWS, ROWS), ROWS)

    def z_send(src, h, dst, lanes, ss, rs):
        def columns(zz):
            return pl.ds(pl.multiple_of((zz * HEADS_HERE + h) * HEAD_DIM, HEAD_DIM), HEAD_DIM)

        for j in ORDER:
            zz = layer(j)
            remote(src.at[:, columns(zz)], dst.at[h, my_rows, lanes], ss, rs, at_layer(zz))
        pltpu.make_async_copy(src.at[:, columns(z)], dst.at[h, my_rows, lanes], rs).start()

    def z_send_kv(h):
        z_send(k_ref, h, zkv, pl.ds(0, HEAD_DIM), zkv_ss.at[h], zkv_rs.at[h])
        z_send(v_ref, h, zkv, pl.ds(HEAD_DIM, HEAD_DIM), zkv_ss.at[h], zkv_rs.at[h])

    def z_send_q(h):
        z_send(q_ref, h, zq, pl.ds(0, HEAD_DIM), zq_ss.at[h], zq_rs.at[h])

    my_share = pl.ds(pl.multiple_of(me * SHARE, SHARE), SHARE)

    def share(o):
        return pl.ds(pl.multiple_of(o * SHARE, SHARE), SHARE)

    def plane_send(src, dst, ss, rs):
        @pl.loop(1, OWNERS)
        def _(j):
            o = peer(j)
            remote(src.at[share(o)], dst.at[my_share], ss, rs, at_owner(o))

        pltpu.make_async_copy(src.at[my_share], dst.at[my_share], rs).start()

    def permute(table, src, dst, block=512):
        @pl.loop(0, TOK_DEV // block)
        def _(i):
            rows = pl.ds(pl.multiple_of(i * block, block), block)
            dst[rows, :] = jnp.dot(
                table[rows, :], src[...], preferred_element_type=jnp.float32
            ).astype(jnp.bfloat16)

    for j in ORDER:
        zz = layer(j)
        remote(meta_ref, zmeta.at[z], zm_ss, zm_rs, at_layer(zz))
    pltpu.make_async_copy(meta_ref, zmeta.at[z], zm_rs).start()
    z_send_kv(0)
    z_send_kv(1)

    bulk_wait(zmeta, zm_rs)

    @pl.loop(0, LAYERS)
    def _(s):
        row = zmeta[s][:, 0:256].astype(jnp.float32)
        wide = jnp.broadcast_to(row, (ROWS, 256))
        diag = iota((ROWS, 256), 0) == iota((ROWS, 256), 1)
        col = jnp.sum(jnp.where(diag, wide, 0.0), axis=1, keepdims=True)
        rank = jnp.sum(jnp.where(wide < col, 1.0, 0.0), axis=1, keepdims=True)
        owner = jnp.floor((col + 0.5) * (1.0 / TOK_DEV))
        pos = owner * (SHARE - 6.0) + rank + (6 * s).astype(jnp.float32)
        rows = pl.ds(pl.multiple_of(s * ROWS, ROWS), ROWS)
        pos_col[rows, :] = jnp.broadcast_to(pos, (ROWS, 128))
        slot_col[rows, :] = jnp.broadcast_to(col, (ROWS, 128))

    def to_row(col_ref, row_ref):
        for b in range(TOK_DEV // 128):
            block = col_ref[b * 128 : (b + 1) * 128, :]
            diag = iota((128, 128), 0) == iota((128, 128), 1)
            row_ref[:, b * 128 : (b + 1) * 128] = jnp.sum(
                jnp.where(diag, block, 0.0), axis=0, keepdims=True
            )

    to_row(pos_col, pos_row)
    to_row(slot_col, slot_row)

    def table_by_row(table, row_ref, sorted_ref):
        @pl.loop(0, TOK_DEV // 64)
        def _(b):
            rows = pl.ds(pl.multiple_of(b * 64, 64), 64)
            want = (iota((64, TOK_DEV), 0) + b * 64).astype(jnp.float32)
            hit = want == row_ref[...]
            table[rows, :] = jnp.where(hit, 1.0, 0.0).astype(jnp.bfloat16)
            if sorted_ref is not None:
                slot = jnp.sum(jnp.where(hit, slot_row[...], 0.0), axis=1, keepdims=True)
                sorted_ref[rows, :] = jnp.broadcast_to(slot, (64, 128))

    def table_by_col(table, col_ref):
        @pl.loop(0, TOK_DEV // 64)
        def _(b):
            rows = pl.ds(pl.multiple_of(b * 64, 64), 64)
            want = iota((64, TOK_DEV), 1).astype(jnp.float32)
            hit = want == col_ref[rows, 0:1]
            table[rows, :] = jnp.where(hit, 1.0, 0.0).astype(jnp.bfloat16)

    table_by_row(p1, pos_row, slot_col)

    def window_of(o):
        return zmeta.at[lax.div(o, 4), :, pl.ds(256, 128)]

    @pl.loop(0, OWNERS)
    def _(o):
        block = slot_col[share(o), :]
        diag = iota((SHARE, 128), 0) == iota((SHARE, 128), 1)
        smeta[o] = jnp.sum(jnp.where(diag, block, 0.0), axis=0, keepdims=True)

    @pl.loop(1, OWNERS)
    def _(j):
        o = peer(j)
        remote(smeta.at[o], ameta.at[me], pm_ss, pm_rs, at_owner(o))
        remote(window_of(o), awin.at[me], pw_ss, pw_rs, at_owner(o))

    pltpu.make_async_copy(smeta.at[me], ameta.at[me], pm_rs).start()
    pltpu.make_async_copy(window_of(me), awin.at[me], pw_rs).start()

    table_by_col(p1t, pos_col)

    bulk_wait(ameta, pm_rs)
    bulk_wait(awin, pw_rs)
    window_row = pltpu.make_async_copy(awin.at[2 * lax.rem(me, 4)], win_smem, win_s)
    window_row.start()

    @pl.loop(0, OWNERS)
    def _(o):
        row = ameta[o]
        wide = jnp.broadcast_to(row, (SHARE, 128))
        diag = iota((SHARE, 128), 0) == iota((SHARE, 128), 1)
        col = jnp.sum(jnp.where(diag, wide, 0.0), axis=1, keepdims=True)
        col = col - (me * TOK_DEV).astype(jnp.float32)
        pos_col[share(o), :] = jnp.broadcast_to(col, (SHARE, 128))

    to_row(pos_col, pos_row)
    table_by_row(p2, pos_row, None)
    table_by_col(p2t, pos_col)
    window_row.wait()

    def sort_kv(h):
        bulk_wait(zkv.at[h], zkv_rs.at[h])
        permute(p1, zkv.at[h], skv.at[h])
        plane_send(skv.at[h], akv.at[h], pkv_ss.at[h], pkv_rs.at[h])

    def sort_q(h):
        bulk_wait(zq.at[h], zq_rs.at[h])
        permute(p1, zq.at[h], sq.at[h])
        plane_send(sq.at[h], aq.at[h], pq_ss.at[h], pq_rs.at[h])

    not_first, not_last = me > 0, me < OWNERS - 1

    def halo_copies(h):
        to_right = pltpu.make_async_remote_copy(
            src_ref=ekv[h].at[pl.ds(REACH + 1, REACH)],
            dst_ref=ekv[h].at[pl.ds(0, REACH)],
            send_sem=h_ss.at[0, h],
            recv_sem=hl_rs.at[h],
            device_id=at_owner(lax.rem(me + 1, OWNERS)),
            device_id_type=MESH,
        )
        to_left = pltpu.make_async_remote_copy(
            src_ref=ekv[h].at[pl.ds(REACH, REACH)],
            dst_ref=ekv[h].at[pl.ds(REACH + TILE_DEV, REACH)],
            send_sem=h_ss.at[1, h],
            recv_sem=hr_rs.at[h],
            device_id=at_owner(lax.rem(me + OWNERS - 1, OWNERS)),
            device_id_type=MESH,
        )
        return to_right, to_left

    def tile_kv(h):
        bulk_wait(akv.at[h], pkv_rs.at[h])

        @pl.loop(0, TILE_DEV)
        def _(t):
            rows = pl.ds(pl.multiple_of(t * TILE, TILE), TILE)
            ekv[h][REACH + t] = jnp.dot(
                p2[rows, :], akv[h], preferred_element_type=jnp.float32
            ).astype(jnp.bfloat16)

        to_right, to_left = halo_copies(h)

        @pl.when(not_last)
        def _():
            to_right.start()

        @pl.when(not_first)
        def _():
            to_left.start()

    def halo_wait(h):
        to_right, to_left = halo_copies(h)

        @pl.when(not_first)
        def _():
            to_right.wait_recv()

        @pl.when(not_last)
        def _():
            to_left.wait_recv()

    factor = HEAD_DIM**-0.5 * LOG2E
    QB = 192

    def attend(h):
        bulk_wait(aq.at[h], pq_rs.at[h])
        permute(p2, aq.at[h], tq)
        halo_wait(h)

        @pl.loop(0, TILE_DEV)
        def _(t):
            starts, biases = [], []
            for w in range(WIN):
                tile = win_smem[0, SHARE + t * WIN + w]
                starts.append(lax.clamp(0, tile - (me * TILE_DEV - REACH), EXT_TILES - 1))
                biases.append(jnp.where(iota((1, TILE), 1) < valid_ref[tile], 0.0, FAR))
            real = valid_ref[me * TILE_DEV + t]
            for b in range(TILE // QB):
                rows = pl.ds(pl.multiple_of(t * TILE + b * QB, QB), QB)
                query = tq[rows, :]
                scores = []
                for w in range(WIN):
                    keys = ekv[h][starts[w], :, 0:HEAD_DIM]
                    scores.append(
                        lax.dot_general(
                            query, keys, (((1,), (1,)), ((), ())), preferred_element_type=jnp.float32
                        )
                        + biases[w]
                    )
                top = functools.reduce(
                    jnp.maximum, [jnp.max(s, axis=1, keepdims=True) for s in scores]
                )
                weights = [jnp.exp2((s - top) * factor) for s in scores]
                total = functools.reduce(
                    jnp.add, [jnp.sum(p, axis=1, keepdims=True) for p in weights]
                )
                mixed = None
                for w in range(WIN):
                    values = ekv[h][starts[w], :, HEAD_DIM : 2 * HEAD_DIM]
                    term = jnp.dot(
                        weights[w].astype(jnp.bfloat16), values, preferred_element_type=jnp.float32
                    )
                    mixed = term if mixed is None else mixed + term
                mixed = mixed / total
                keep = iota((QB, 1), 0) + b * QB < real
                ot[rows, :] = jnp.where(keep, mixed, 0.0).astype(jnp.bfloat16)

        permute(p2t, ot, oa.at[h])
        plane_send(oa.at[h], ox.at[h], po_ss.at[h], po_rs.at[h])

    def give_back(h):
        bulk_wait(ox.at[h], po_rs.at[h])
        permute(p1t, ox.at[h], orr.at[h])
        columns = pl.ds(pl.multiple_of((z * HEADS_HERE + h) * HEAD_DIM, HEAD_DIM), HEAD_DIM)
        for j in ORDER:
            zz = layer(j)
            rows = pl.ds(pl.multiple_of(zz * ROWS, ROWS), ROWS)
            remote(orr.at[h, rows], out_ref.at[:, columns], zo_ss.at[h], zo_rs.at[h], at_layer(zz))
        pltpu.make_async_copy(orr.at[h, my_rows], out_ref.at[:, columns], zo_rs.at[h]).start()

    sort_kv(0)
    z_send_kv(2)
    tile_kv(0)
    sort_kv(1)
    z_send_q(0)
    z_send_q(1)
    tile_kv(1)
    sort_kv(2)
    z_send_q(2)
    sort_q(0)
    tile_kv(2)
    sort_q(1)
    attend(0)
    sort_q(2)
    give_back(0)
    attend(1)
    give_back(1)
    attend(2)
    give_back(2)

    bulk_wait(zmeta.at[pl.ds(0, LAYERS - 1)], zm_ss)
    bulk_wait(smeta.at[pl.ds(0, OWNERS - 1)], pm_ss)
    bulk_wait(awin.at[pl.ds(0, OWNERS - 1)], pw_ss)
    z_sent = pl.ds(0, (LAYERS - 1) * ROWS)
    plane_sent = pl.ds(0, (OWNERS - 1) * SHARE)
    for h in range(HEADS_HERE):
        bulk_wait(zkv.at[h, z_sent], zkv_ss.at[h])
        bulk_wait(zq.at[h, z_sent], zq_ss.at[h])
        bulk_wait(skv.at[h, plane_sent], pkv_ss.at[h])
        bulk_wait(sq.at[h, plane_sent], pq_ss.at[h])
        bulk_wait(oa.at[h, plane_sent], po_ss.at[h])
        bulk_wait(orr.at[h, z_sent], zo_ss.at[h])
        to_right, to_left = halo_copies(h)

        @pl.when(not_last)
        def _():
            to_right.wait_send()

        @pl.when(not_first)
        def _():
            to_left.wait_send()

        bulk_wait(out_ref.at[:, pl.ds(0, LAYERS * HEAD_DIM)], zo_rs.at[h])


def body(query, key, value, raster_to_tile, window_list, valid_count):
    meta = jnp.concatenate(
        [
            raster_to_tile,
            jnp.full((256 - ROWS,), 1 << 20, jnp.int32),
            jnp.zeros((SHARE,), jnp.int32),
            window_list.reshape(-1),
            jnp.zeros((128 - SHARE - TILE_DEV * WIN,), jnp.int32),
        ]
    ).reshape(1, 384)
    heads, bf16, dma = HEADS_HERE, jnp.bfloat16, pltpu.SemaphoreType.DMA
    vmem = pltpu.VMEM
    kv, one = 2 * HEAD_DIM, HEAD_DIM
    scratch = [
        vmem((heads, TOK_DEV, kv), bf16),
        vmem((heads, TOK_DEV, one), bf16),
        vmem((LAYERS, 1, 384), jnp.int32),
        vmem((heads, TOK_DEV, kv), bf16),
        vmem((heads, TOK_DEV, one), bf16),
        vmem((heads, TOK_DEV, kv), bf16),
        vmem((heads, TOK_DEV, one), bf16),
        vmem((EXT_TILES, TILE, kv), bf16),
        vmem((EXT_TILES, TILE, kv), bf16),
        vmem((EXT_TILES, TILE, kv), bf16),
        vmem((TOK_DEV, one), bf16),
        vmem((TOK_DEV, one), bf16),
        vmem((heads, TOK_DEV, one), bf16),
        vmem((heads, TOK_DEV, one), bf16),
        vmem((heads, TOK_DEV, one), bf16),
        vmem((OWNERS, 1, 128), jnp.float32),
        vmem((OWNERS, 1, 128), jnp.float32),
        vmem((OWNERS, 1, 128), jnp.int32),
        pltpu.SMEM((1, 128), jnp.int32),
        vmem((TOK_DEV, 128), jnp.float32),
        vmem((TOK_DEV, 128), jnp.float32),
        vmem((1, TOK_DEV), jnp.float32),
        vmem((1, TOK_DEV), jnp.float32),
        vmem((TOK_DEV, TOK_DEV), bf16),
        vmem((TOK_DEV, TOK_DEV), bf16),
        vmem((TOK_DEV, TOK_DEV), bf16),
        vmem((TOK_DEV, TOK_DEV), bf16),
        dma((heads,)), dma((heads,)), dma((heads,)), dma((heads,)), dma, dma,
        dma((heads,)), dma((heads,)), dma((heads,)), dma((heads,)), dma, dma,
        dma((2, heads)), dma((heads,)), dma((heads,)),
        dma((heads,)), dma((heads,)), dma((heads,)), dma((heads,)), dma, dma, dma,
    ]
    anywhere = pl.BlockSpec(memory_space=pl.ANY)
    return pl.pallas_call(
        kernel,
        out_shape=jax.ShapeDtypeStruct(query.shape, query.dtype),
        in_specs=[
            pl.BlockSpec(memory_space=pltpu.SMEM),
            anywhere,
            anywhere,
            anywhere,
            pl.BlockSpec(memory_space=vmem),
        ],
        out_specs=anywhere,
        scratch_shapes=scratch,
        compiler_params=pltpu.CompilerParams(
            collective_id=0, has_side_effects=True, vmem_limit_bytes=58 * 2**20
        ),
    )(valid_count, query, key, value, meta)


def solution(mesh):
    placed = (
        P(("seq", "head"), None),
        P(("seq", "head"), None),
        P(("seq", "head"), None),
        P(("seq", "head")),
        P("seq", None),
        P(),
    )
    return jax.shard_map(
        body, mesh=mesh, in_specs=placed, out_specs=P(("seq", "head"), None), check_vma=False
    )
```

time: 557 us -> 166 us (0.30)
  waiting for transfers between devices: 238 us -> 0 us
  local copies, waits for them, and re-layouts: 182 us -> 4.45 us
  Pallas kernels: 0 us -> 161 us
  blocking collectives: 61.3 us -> 0 us
  starting transfers between devices: 37.9 us -> 0 us
  other arithmetic: 17.9 us -> 0 us
  matrix products: 16.8 us -> 0 us
    all_to_all x6 -> x0, waiting for transfers between devices: 238 us -> none  [the longest x1 153 us: body(): lax.all_to_all(wide_pair, 'seq', split_axis=0, concat_axis=0, tiled=True)]
    pallas_call x0 -> x1, Pallas kernels: none -> 161 us  [body(): pl.pallas_call(kernel, out_shape=jax.ShapeDtypeStruct(query.shape, query....]
    gather x16 -> x0, local copies, waits for them, and re-layouts: 72.6 us -> none  [the longest x4 32.2 us: one_tile(): picked = pair_blocks[windows]]
    all_to_all x2 -> x0, blocking collectives: 61.3 us -> none  [the longest x1 40.7 us: body(): lax.all_to_all(outgoing, 'seq', split_axis=0, concat_axis=0, tiled=True)]
    all_to_all x6 -> x0, starting transfers between devices: 37.9 us -> none  [the longest x1 9.14 us: body(): lax.all_to_all(lax.all_to_all(query_sorted, 'seq', split_axis=0, concat_a...]
    reshape x7 -> x2, local copies, waits for them, and re-layouts: 33.4 us -> 1.33 us  [the longest x1 0.76 us: body(): window_list.reshape(-1)]
    scatter x3 -> x0, local copies, waits for them, and re-layouts: 24.9 us -> none  [the longest x1 17.6 us: body(): place_ext = jnp.full((ext_rows,), 3 * tok_dev, jnp.int32).at[target].set(...]
    all_to_all x8 -> x0, local copies, waits for them, and re-layouts: 24.8 us -> none  [the longest x1 10.9 us: body(): lax.all_to_all(lax.all_to_all(wide_pair, 'seq', split_axis=0, concat_axis...]
  transfers between devices with their start and end apart: 6 -> 0, of which waited for: 6 -> 0; matrix products, arithmetic and copies ran while one was open for 11% -> 0% of each run, Pallas kernels for 0% -> 0%
where the time goes in v1:
time: 166 us
  Pallas kernels  161 us (97%)
  local copies, waits for them, and re-layouts  4.45 us (3%)
    pallas_call x1, Pallas kernels, body(): pl.pallas_call(kernel, out_shape=jax.ShapeDtypeStruct(query.shape, query....  161 us

profile of v1, /device:TPU:1, one launch (start us, length us, event | category | flops | bytes accessed | tf_op | source)
XLA Modules:
  0.0 165.8 jit_solution(13470795480968018843)
XLA Ops:
  0.0 0.8 reshape.6
  0.8 0.8 concatenate.3
  1.5 0.6 reshape.7.meta_ref
  2.1 161.3 %shard_map.64 = bf16[192,3072]{1,0:T(8,128)(2,1)} custom-call(s32[128]{0:T(128)} %valid_ref.1, bf16[192,3072]{1,0:T(8,128)(2,1)} %q_ref.1, bf16[192,3072]{1,0:T(8,128)(2,1)} %k_ref.1, bf16[192,3072]{1,0:T(8,128)(2,1)} %v_ref.1, s32[1,384]{1,0:T(1,128)} %reshape.7.meta_ref), custom_call_target="tpu_custom_call" | custom-call | tf_op jit(solution)/shard_map/pallas_call | solution.py:436
  163.4 2.4 %copy.8 = bf16[192,3072]{1,0:T(8,128)(2,1)} copy(bf16[192,3072]{1,0:T(8,128)(2,1)} %shard_map.64) | data formatting | bytes 2359296
  (3 shorter events, 0.0 us)

commit v2 on v1

--- a/solution.py
+++ b/solution.py
@@ -44,15 +44,14 @@
 
 
 def kernel(
-    valid_ref, q_ref, k_ref, v_ref, meta_ref, out_ref,
-    zkv, zq, zmeta, skv, sq, akv, aq, ekv0, ekv1, ekv2, tq, ot, oa, ox, orr,
-    smeta, ameta, awin, win_smem, pos_col, slot_col, pos_row, slot_row,
+    valid_ref, q_ref, k_ref, v_ref, slots_ref, windows_ref, out_ref,
+    zkv, zq, zmeta, zwin, skv, sq, akv, aq, ekv, ekw, tq, ot, oa, ox, orr,
+    smeta, ameta, awin, win_smem, pos_col, slot_col, pos_row, slot_row, tile_col, tile_row,
     p1, p1t, p2, p2t,
     zkv_ss, zkv_rs, zq_ss, zq_rs, zm_ss, zm_rs,
     pkv_ss, pkv_rs, pq_ss, pq_rs, pm_ss, pm_rs,
-    h_ss, hl_rs, hr_rs, po_ss, po_rs, zo_ss, zo_rs, win_s, pw_ss, pw_rs,
+    h_ss, hl_rs, hr_rs, po_ss, po_rs, zo_ss, zo_rs, win_s, pw_ss, pw_rs, zw_ss, zw_rs,
 ):
-    ekv = (ekv0, ekv1, ekv2)
     seq, head = lax.axis_index("seq"), lax.axis_index("head")
     z, y = lax.div(seq, 4), lax.rem(seq, 4)
     x, core = lax.div(head, 2), lax.rem(head, 2)
@@ -119,28 +118,45 @@
 
         pltpu.make_async_copy(src.at[my_share], dst.at[my_share], rs).start()
 
-    def permute(table, src, dst, block=512):
+    def permute(table, src, store, block=512, depth=256):
         @pl.loop(0, TOK_DEV // block)
         def _(i):
             rows = pl.ds(pl.multiple_of(i * block, block), block)
-            dst[rows, :] = jnp.dot(
-                table[rows, :], src[...], preferred_element_type=jnp.float32
-            ).astype(jnp.bfloat16)
+            total = None
+            for k in range(0, TOK_DEV, depth):
+                term = jnp.dot(
+                    table[rows, k : k + depth],
+                    src[k : k + depth, :],
+                    preferred_element_type=jnp.float32,
+                )
+                total = term if total is None else total + term
+            store(i, rows, total.astype(jnp.bfloat16))
+
+    def into(ref):
+        def store(i, rows, value):
+            ref[rows, :] = value
+
+        return store
 
     for j in ORDER:
         zz = layer(j)
-        remote(meta_ref, zmeta.at[z], zm_ss, zm_rs, at_layer(zz))
-    pltpu.make_async_copy(meta_ref, zmeta.at[z], zm_rs).start()
+        remote(slots_ref, zmeta.at[z], zm_ss, zm_rs, at_layer(zz))
+        remote(windows_ref, zwin.at[z], zw_ss, zw_rs, at_layer(zz))
+    pltpu.make_async_copy(slots_ref, zmeta.at[z], zm_rs).start()
+    pltpu.make_async_copy(windows_ref, zwin.at[z], zw_rs).start()
     z_send_kv(0)
+    z_send_q(0)
     z_send_kv(1)
+    z_send_q(1)
+    z_send_kv(2)
+    z_send_q(2)
 
     bulk_wait(zmeta, zm_rs)
 
     @pl.loop(0, LAYERS)
     def _(s):
-        row = zmeta[s][:, 0:256].astype(jnp.float32)
-        wide = jnp.broadcast_to(row, (ROWS, 256))
-        diag = iota((ROWS, 256), 0) == iota((ROWS, 256), 1)
+        wide = jnp.broadcast_to(zmeta[s].astype(jnp.float32), (ROWS, ROWS))
+        diag = iota((ROWS, ROWS), 0) == iota((ROWS, ROWS), 1)
         col = jnp.sum(jnp.where(diag, wide, 0.0), axis=1, keepdims=True)
         rank = jnp.sum(jnp.where(wide < col, 1.0, 0.0), axis=1, keepdims=True)
         owner = jnp.floor((col + 0.5) * (1.0 / TOK_DEV))
@@ -179,71 +195,77 @@
             hit = want == col_ref[rows, 0:1]
             table[rows, :] = jnp.where(hit, 1.0, 0.0).astype(jnp.bfloat16)
 
-    table_by_row(p1, pos_row, slot_col)
-
     def window_of(o):
-        return zmeta.at[lax.div(o, 4), :, pl.ds(256, 128)]
-
-    @pl.loop(0, OWNERS)
-    def _(o):
-        block = slot_col[share(o), :]
-        diag = iota((SHARE, 128), 0) == iota((SHARE, 128), 1)
-        smeta[o] = jnp.sum(jnp.where(diag, block, 0.0), axis=0, keepdims=True)
-
-    @pl.loop(1, OWNERS)
-    def _(j):
-        o = peer(j)
-        remote(smeta.at[o], ameta.at[me], pm_ss, pm_rs, at_owner(o))
-        remote(window_of(o), awin.at[me], pw_ss, pw_rs, at_owner(o))
-
-    pltpu.make_async_copy(smeta.at[me], ameta.at[me], pm_rs).start()
-    pltpu.make_async_copy(window_of(me), awin.at[me], pw_rs).start()
-
-    table_by_col(p1t, pos_col)
-
-    bulk_wait(ameta, pm_rs)
-    bulk_wait(awin, pw_rs)
+        return zwin.at[lax.div(o, 4)]
+
     window_row = pltpu.make_async_copy(awin.at[2 * lax.rem(me, 4)], win_smem, win_s)
-    window_row.start()
-
-    @pl.loop(0, OWNERS)
-    def _(o):
-        row = ameta[o]
-        wide = jnp.broadcast_to(row, (SHARE, 128))
-        diag = iota((SHARE, 128), 0) == iota((SHARE, 128), 1)
-        col = jnp.sum(jnp.where(diag, wide, 0.0), axis=1, keepdims=True)
-        col = col - (me * TOK_DEV).astype(jnp.float32)
-        pos_col[share(o), :] = jnp.broadcast_to(col, (SHARE, 128))
-
-    to_row(pos_col, pos_row)
-    table_by_row(p2, pos_row, None)
-    table_by_col(p2t, pos_col)
-    window_row.wait()
+
+    def send_slots():
+        table_by_row(p1, pos_row, slot_col)
+        bulk_wait(zwin, zw_rs)
+
+        @pl.loop(0, OWNERS)
+        def _(o):
+            block = slot_col[share(o), :]
+            diag = iota((SHARE, 128), 0) == iota((SHARE, 128), 1)
+            smeta[o] = jnp.sum(jnp.where(diag, block, 0.0), axis=0, keepdims=True)
+
+        @pl.loop(1, OWNERS)
+        def _(j):
+            o = peer(j)
+            remote(smeta.at[o], ameta.at[me], pm_ss, pm_rs, at_owner(o))
+            remote(window_of(o), awin.at[me], pw_ss, pw_rs, at_owner(o))
+
+        pltpu.make_async_copy(smeta.at[me], ameta.at[me], pm_rs).start()
+        pltpu.make_async_copy(window_of(me), awin.at[me], pw_rs).start()
+
+    def take_slots():
+        bulk_wait(ameta, pm_rs)
+        bulk_wait(awin, pw_rs)
+        window_row.start()
+
+        @pl.loop(0, OWNERS)
+        def _(o):
+            wide = jnp.broadcast_to(ameta[o], (SHARE, 128))
+            diag = iota((SHARE, 128), 0) == iota((SHARE, 128), 1)
+            col = jnp.sum(jnp.where(diag, wide, 0.0), axis=1, keepdims=True)
+            col = col - (me * TOK_DEV).astype(jnp.float32)
+            tile_col[share(o), :] = jnp.broadcast_to(col, (SHARE, 128))
+
+        to_row(tile_col, tile_row)
+        table_by_row(p2, tile_row, None)
+        window_row.wait()
+
+    def back_from_tiles():
+        table_by_col(p2t, tile_col)
+
+    def back_from_owners():
+        table_by_col(p1t, pos_col)
 
     def sort_kv(h):
         bulk_wait(zkv.at[h], zkv_rs.at[h])
-        permute(p1, zkv.at[h], skv.at[h])
+        permute(p1, zkv.at[h], into(skv.at[h]))
         plane_send(skv.at[h], akv.at[h], pkv_ss.at[h], pkv_rs.at[h])
 
     def sort_q(h):
         bulk_wait(zq.at[h], zq_rs.at[h])
-        permute(p1, zq.at[h], sq.at[h])
+        permute(p1, zq.at[h], into(sq.at[h]))
         plane_send(sq.at[h], aq.at[h], pq_ss.at[h], pq_rs.at[h])
 
     not_first, not_last = me > 0, me < OWNERS - 1
 
     def halo_copies(h):
         to_right = pltpu.make_async_remote_copy(
-            src_ref=ekv[h].at[pl.ds(REACH + 1, REACH)],
-            dst_ref=ekv[h].at[pl.ds(0, REACH)],
+            src_ref=ekv.at[h, pl.ds(REACH + 1, REACH)],
+            dst_ref=ekv.at[h, pl.ds(0, REACH)],
             send_sem=h_ss.at[0, h],
             recv_sem=hl_rs.at[h],
             device_id=at_owner(lax.rem(me + 1, OWNERS)),
             device_id_type=MESH,
         )
         to_left = pltpu.make_async_remote_copy(
-            src_ref=ekv[h].at[pl.ds(REACH, REACH)],
-            dst_ref=ekv[h].at[pl.ds(REACH + TILE_DEV, REACH)],
+            src_ref=ekv.at[h, pl.ds(REACH, REACH)],
+            dst_ref=ekv.at[h, pl.ds(REACH + TILE_DEV, REACH)],
             send_sem=h_ss.at[1, h],
             recv_sem=hr_rs.at[h],
             device_id=at_owner(lax.rem(me + OWNERS - 1, OWNERS)),
@@ -254,13 +276,10 @@
     def tile_kv(h):
         bulk_wait(akv.at[h], pkv_rs.at[h])
 
-        @pl.loop(0, TILE_DEV)
-        def _(t):
-            rows = pl.ds(pl.multiple_of(t * TILE, TILE), TILE)
-            ekv[h][REACH + t] = jnp.dot(
-                p2[rows, :], akv[h], preferred_element_type=jnp.float32
-            ).astype(jnp.bfloat16)
-
+        def store(t, rows, value):
+            ekv[h, REACH + t] = value
+
+        permute(p2, akv.at[h], store, block=TILE)
         to_right, to_left = halo_copies(h)
 
         @pl.when(not_last)
@@ -283,57 +302,64 @@
             to_left.wait_recv()
 
     factor = HEAD_DIM**-0.5 * LOG2E
-    QB = 192
+
+    def tile_q(h):
+        bulk_wait(aq.at[h], pq_rs.at[h])
+        permute(p2, aq.at[h], into(tq.at[h]))
 
     def attend(h):
-        bulk_wait(aq.at[h], pq_rs.at[h])
-        permute(p2, aq.at[h], tq)
         halo_wait(h)
+
+        @pl.loop(0, EXT_TILES)
+        def _(e):
+            ekw[e] = ekv[h, e]
 
         @pl.loop(0, TILE_DEV)
         def _(t):
             starts, biases = [], []
             for w in range(WIN):
-                tile = win_smem[0, SHARE + t * WIN + w]
+                tile = win_smem[t, w]
                 starts.append(lax.clamp(0, tile - (me * TILE_DEV - REACH), EXT_TILES - 1))
                 biases.append(jnp.where(iota((1, TILE), 1) < valid_ref[tile], 0.0, FAR))
             real = valid_ref[me * TILE_DEV + t]
-            for b in range(TILE // QB):
-                rows = pl.ds(pl.multiple_of(t * TILE + b * QB, QB), QB)
-                query = tq[rows, :]
-                scores = []
-                for w in range(WIN):
-                    keys = ekv[h][starts[w], :, 0:HEAD_DIM]
-                    scores.append(
-                        lax.dot_general(
-                            query, keys, (((1,), (1,)), ((), ())), preferred_element_type=jnp.float32
-                        )
-                        + biases[w]
+            rows = pl.ds(pl.multiple_of(t * TILE, TILE), TILE)
+            query = tq[h, rows, :]
+            scores = []
+            for w in range(WIN):
+                keys = ekw[starts[w], :, 0:HEAD_DIM]
+                scores.append(
+                    lax.dot_general(
+                        query, keys, (((1,), (1,)), ((), ())), preferred_element_type=jnp.float32
                     )
-                top = functools.reduce(
-                    jnp.maximum, [jnp.max(s, axis=1, keepdims=True) for s in scores]
+                    + biases[w]
                 )
-                weights = [jnp.exp2((s - top) * factor) for s in scores]
-                total = functools.reduce(
-                    jnp.add, [jnp.sum(p, axis=1, keepdims=True) for p in weights]
+            top = functools.reduce(
+                jnp.maximum, [jnp.max(s, axis=1, keepdims=True) for s in scores]
+            )
+            weights = [jnp.exp2((s - top) * factor) for s in scores]
+            total = functools.reduce(
+                jnp.add, [jnp.sum(p, axis=1, keepdims=True) for p in weights]
+            )
+            mixed = None
+            for w in range(WIN):
+                values = ekw[starts[w], :, HEAD_DIM : 2 * HEAD_DIM]
+                term = jnp.dot(
+                    weights[w].astype(jnp.bfloat16), values, preferred_element_type=jnp.float32
                 )
-                mixed = None
-                for w in range(WIN):
-                    values = ekv[h][starts[w], :, HEAD_DIM : 2 * HEAD_DIM]
-                    term = jnp.dot(
-                        weights[w].astype(jnp.bfloat16), values, preferred_element_type=jnp.float32
-                    )
-                    mixed = term if mixed is None else mixed + term
-                mixed = mixed / total
-                keep = iota((QB, 1), 0) + b * QB < real
-                ot[rows, :] = jnp.where(keep, mixed, 0.0).astype(jnp.bfloat16)
-
-        permute(p2t, ot, oa.at[h])
+                mixed = term if mixed is None else mixed + term
+            mixed = mixed / total
+            keep = iota((TILE, 1), 0) < real
+            ot[rows, :] = jnp.where(keep, mixed, 0.0).astype(jnp.bfloat16)
+
+    def send_back(h):
+        permute(p2t, ot, into(oa.at[h]))
         plane_send(oa.at[h], ox.at[h], po_ss.at[h], po_rs.at[h])
 
+    def unsort(h):
+        bulk_wait(ox.at[h], po_rs.at[h])
+        permute(p1t, ox.at[h], into(orr.at[h]))
+
     def give_back(h):
-        bulk_wait(ox.at[h], po_rs.at[h])
-        permute(p1t, ox.at[h], orr.at[h])
         columns = pl.ds(pl.multiple_of((z * HEADS_HERE + h) * HEAD_DIM, HEAD_DIM), HEAD_DIM)
         for j in ORDER:
             zz = layer(j)
@@ -341,27 +367,37 @@
             remote(orr.at[h, rows], out_ref.at[:, columns], zo_ss.at[h], zo_rs.at[h], at_layer(zz))
         pltpu.make_async_copy(orr.at[h, my_rows], out_ref.at[:, columns], zo_rs.at[h]).start()
 
+    send_slots()
+    take_slots()
     sort_kv(0)
-    z_send_kv(2)
+    back_from_tiles()
+    back_from_owners()
+    sort_q(0)
     tile_kv(0)
+    tile_q(0)
     sort_kv(1)
-    z_send_q(0)
-    z_send_q(1)
+    attend(0)
+    send_back(0)
+    sort_q(1)
     tile_kv(1)
+    tile_q(1)
+    unsort(0)
     sort_kv(2)
-    z_send_q(2)
-    sort_q(0)
-    tile_kv(2)
-    sort_q(1)
-    attend(0)
+    attend(1)
     sort_q(2)
     give_back(0)
-    attend(1)
+    tile_kv(2)
+    tile_q(2)
+    send_back(1)
+    attend(2)
+    send_back(2)
+    unsort(1)
     give_back(1)
-    attend(2)
+    unsort(2)
     give_back(2)
 
     bulk_wait(zmeta.at[pl.ds(0, LAYERS - 1)], zm_ss)
+    bulk_wait(zwin.at[pl.ds(0, LAYERS - 1)], zw_ss)
     bulk_wait(smeta.at[pl.ds(0, OWNERS - 1)], pm_ss)
     bulk_wait(awin.at[pl.ds(0, OWNERS - 1)], pw_ss)
     z_sent = pl.ds(0, (LAYERS - 1) * ROWS)
@@ -387,41 +423,34 @@
 
 
 def body(query, key, value, raster_to_tile, window_list, valid_count):
-    meta = jnp.concatenate(
-        [
-            raster_to_tile,
-            jnp.full((256 - ROWS,), 1 << 20, jnp.int32),
-            jnp.zeros((SHARE,), jnp.int32),
-            window_list.reshape(-1),
-            jnp.zeros((128 - SHARE - TILE_DEV * WIN,), jnp.int32),
-        ]
-    ).reshape(1, 384)
     heads, bf16, dma = HEADS_HERE, jnp.bfloat16, pltpu.SemaphoreType.DMA
     vmem = pltpu.VMEM
     kv, one = 2 * HEAD_DIM, HEAD_DIM
     scratch = [
         vmem((heads, TOK_DEV, kv), bf16),
         vmem((heads, TOK_DEV, one), bf16),
-        vmem((LAYERS, 1, 384), jnp.int32),
+        vmem((LAYERS, 1, ROWS), jnp.int32),
+        vmem((LAYERS, TILE_DEV, WIN), jnp.int32),
         vmem((heads, TOK_DEV, kv), bf16),
         vmem((heads, TOK_DEV, one), bf16),
         vmem((heads, TOK_DEV, kv), bf16),
         vmem((heads, TOK_DEV, one), bf16),
+        vmem((heads, EXT_TILES, TILE, kv), bf16),
         vmem((EXT_TILES, TILE, kv), bf16),
-        vmem((EXT_TILES, TILE, kv), bf16),
-        vmem((EXT_TILES, TILE, kv), bf16),
-        vmem((TOK_DEV, one), bf16),
+        vmem((heads, TOK_DEV, one), bf16),
         vmem((TOK_DEV, one), bf16),
         vmem((heads, TOK_DEV, one), bf16),
         vmem((heads, TOK_DEV, one), bf16),
         vmem((heads, TOK_DEV, one), bf16),
         vmem((OWNERS, 1, 128), jnp.float32),
         vmem((OWNERS, 1, 128), jnp.float32),
-        vmem((OWNERS, 1, 128), jnp.int32),
-        pltpu.SMEM((1, 128), jnp.int32),
+        vmem((OWNERS, TILE_DEV, WIN), jnp.int32),
+        pltpu.SMEM((TILE_DEV, WIN), jnp.int32),
         vmem((TOK_DEV, 128), jnp.float32),
         vmem((TOK_DEV, 128), jnp.float32),
         vmem((1, TOK_DEV), jnp.float32),
+        vmem((1, TOK_DEV), jnp.float32),
+        vmem((TOK_DEV, 128), jnp.float32),
         vmem((1, TOK_DEV), jnp.float32),
         vmem((TOK_DEV, TOK_DEV), bf16),
         vmem((TOK_DEV, TOK_DEV), bf16),
@@ -430,7 +459,7 @@
         dma((heads,)), dma((heads,)), dma((heads,)), dma((heads,)), dma, dma,
         dma((heads,)), dma((heads,)), dma((heads,)), dma((heads,)), dma, dma,
         dma((2, heads)), dma((heads,)), dma((heads,)),
-        dma((heads,)), dma((heads,)), dma((heads,)), dma((heads,)), dma, dma, dma,
+        dma((heads,)), dma((heads,)), dma((heads,)), dma((heads,)), dma, dma, dma, dma, dma,
     ]
     anywhere = pl.BlockSpec(memory_space=pl.ANY)
     return pl.pallas_call(
@@ -442,13 +471,14 @@
             anywhere,
             anywhere,
             pl.BlockSpec(memory_space=vmem),
+            pl.BlockSpec(memory_space=vmem),
         ],
         out_specs=anywhere,
         scratch_shapes=scratch,
         compiler_params=pltpu.CompilerParams(
             collective_id=0, has_side_effects=True, vmem_limit_bytes=58 * 2**20
         ),
-    )(valid_count, query, key, value, meta)
+    )(valid_count, query, key, value, raster_to_tile.reshape(1, ROWS), window_list)
 
 
 def solution(mesh):

time: 166 us -> 141 us (0.85)
  Pallas kernels: 161 us -> 139 us
  local copies, waits for them, and re-layouts: 4.45 us -> 2.36 us
    pallas_call x1, Pallas kernels: 161 us -> 139 us  [body(): pl.pallas_call(kernel, out_shape=jax.ShapeDtypeStruct(query.shape, query....]
where the time goes in v2:
time: 141 us
  Pallas kernels  139 us (99%)
  local copies, waits for them, and re-layouts  2.36 us (2%)
    pallas_call x1, Pallas kernels, body(): pl.pallas_call(kernel, out_shape=jax.ShapeDtypeStruct(query.shape, query....  139 us

profile of v2, /device:TPU:1, one launch (start us, length us, event | category | flops | bytes accessed | tf_op | source)
XLA Modules:
  0.0 140.9 jit_solution(15114063710623431742)
XLA Ops:
  0.0 138.6 %shard_map.64 = bf16[192,3072]{1,0:T(8,128)(2,1)} custom-call(s32[128]{0:T(128)} %valid_ref.1, bf16[192,3072]{1,0:T(8,128)(2,1)} %q_ref.1, bf16[192,3072]{1,0:T(8,128)(2,1)} %k_ref.1, bf16[192,3072]{1,0:T(8,128)(2,1)} %v_ref.1, s32[1,192]{1,0:T(1,128)} %bitcast.1, s32[4,4]{1,0:T(4,128)} %windows_ref.1), custom_call_target="tpu_custom_call" | custom-call | tf_op jit(solution)/shard_map/pallas_call | solution.py:465
  138.6 2.4 %copy.8 = bf16[192,3072]{1,0:T(8,128)(2,1)} copy(bf16[192,3072]{1,0:T(8,128)(2,1)} %shard_map.64) | data formatting | bytes 2359296

commit v3 on v2

--- a/solution.py
+++ b/solution.py
@@ -110,17 +110,28 @@
     def share(o):
         return pl.ds(pl.multiple_of(o * SHARE, SHARE), SHARE)
 
-    def plane_send(src, dst, ss, rs):
-        @pl.loop(1, OWNERS)
-        def _(j):
-            o = peer(j)
-            remote(src.at[share(o)], dst.at[my_share], ss, rs, at_owner(o))
-
-        pltpu.make_async_copy(src.at[my_share], dst.at[my_share], rs).start()
-
-    def permute(table, src, store, block=512, depth=256):
+    def permute_send(table, src, stage, dst, ss, rs, owners=8):
+        def store(i, rows, value):
+            stage[rows, :] = value
+
+            @pl.loop(0, owners)
+            def _(j):
+                o = i * owners + lax.rem(me + 1 + j, owners)
+
+                @pl.when(o != me)
+                def _():
+                    remote(stage.at[share(o)], dst.at[my_share], ss, rs, at_owner(o))
+
+                @pl.when(o == me)
+                def _():
+                    pltpu.make_async_copy(stage.at[my_share], dst.at[my_share], rs).start()
+
+        permute(table, src, store, block=owners * SHARE, first=lax.div(me, owners))
+
+    def permute(table, src, store, block=512, depth=256, first=0):
         @pl.loop(0, TOK_DEV // block)
-        def _(i):
+        def _(step):
+            i = lax.rem(step + first, TOK_DEV // block)
             rows = pl.ds(pl.multiple_of(i * block, block), block)
             total = None
             for k in range(0, TOK_DEV, depth):
@@ -244,13 +255,11 @@
 
     def sort_kv(h):
         bulk_wait(zkv.at[h], zkv_rs.at[h])
-        permute(p1, zkv.at[h], into(skv.at[h]))
-        plane_send(skv.at[h], akv.at[h], pkv_ss.at[h], pkv_rs.at[h])
+        permute_send(p1, zkv.at[h], skv.at[h], akv.at[h], pkv_ss.at[h], pkv_rs.at[h])
 
     def sort_q(h):
         bulk_wait(zq.at[h], zq_rs.at[h])
-        permute(p1, zq.at[h], into(sq.at[h]))
-        plane_send(sq.at[h], aq.at[h], pq_ss.at[h], pq_rs.at[h])
+        permute_send(p1, zq.at[h], sq.at[h], aq.at[h], pq_ss.at[h], pq_rs.at[h])
 
     not_first, not_last = me > 0, me < OWNERS - 1
 
@@ -352,8 +361,7 @@
             ot[rows, :] = jnp.where(keep, mixed, 0.0).astype(jnp.bfloat16)
 
     def send_back(h):
-        permute(p2t, ot, into(oa.at[h]))
-        plane_send(oa.at[h], ox.at[h], po_ss.at[h], po_rs.at[h])
+        permute_send(p2t, ot, oa.at[h], ox.at[h], po_ss.at[h], po_rs.at[h])
 
     def unsort(h):
         bulk_wait(ox.at[h], po_rs.at[h])
@@ -366,6 +374,30 @@
             rows = pl.ds(pl.multiple_of(zz * ROWS, ROWS), ROWS)
             remote(orr.at[h, rows], out_ref.at[:, columns], zo_ss.at[h], zo_rs.at[h], at_layer(zz))
         pltpu.make_async_copy(orr.at[h, my_rows], out_ref.at[:, columns], zo_rs.at[h]).start()
+
+    def unsort_give_back(h):
+        bulk_wait(ox.at[h], po_rs.at[h])
+        columns = pl.ds(pl.multiple_of((z * HEADS_HERE + h) * HEAD_DIM, HEAD_DIM), HEAD_DIM)
+
+        def store(i, rows, value):
+            orr[h, rows, :] = value
+            for j in range(2):
+                zz = i * 2 + j
+                part = pl.ds(pl.multiple_of(zz * ROWS, ROWS), ROWS)
+
+                @pl.when(zz != z)
+                def _():
+                    remote(
+                        orr.at[h, part], out_ref.at[:, columns], zo_ss.at[h], zo_rs.at[h], at_layer(zz)
+                    )
+
+                @pl.when(zz == z)
+                def _():
+                    pltpu.make_async_copy(
+                        orr.at[h, my_rows], out_ref.at[:, columns], zo_rs.at[h]
+                    ).start()
+
+        permute(p1t, ox.at[h], store, block=2 * ROWS, first=lax.div(layer(4), 2))
 
     send_slots()
     take_slots()
@@ -391,10 +423,8 @@
     send_back(1)
     attend(2)
     send_back(2)
-    unsort(1)
-    give_back(1)
-    unsort(2)
-    give_back(2)
+    unsort_give_back(1)
+    unsort_give_back(2)
 
     bulk_wait(zmeta.at[pl.ds(0, LAYERS - 1)], zm_ss)
     bulk_wait(zwin.at[pl.ds(0, LAYERS - 1)], zw_ss)

time: 141 us -> 138 us (0.979)
  Pallas kernels: 139 us -> 135 us
    pallas_call x1, Pallas kernels: 139 us -> 135 us  [body(): pl.pallas_call(kernel, out_shape=jax.ShapeDtypeStruct(query.shape, query....]
where the time goes in v3:
time: 138 us; the launch traced here: 137 us
  Pallas kernels  135 us (98%)
  local copies, waits for them, and re-layouts  2.36 us (2%)
    pallas_call x1, Pallas kernels, body(): pl.pallas_call(kernel, out_shape=jax.ShapeDtypeStruct(query.shape, query....  135 us

profile of v3, /device:TPU:1, one launch (start us, length us, event | category | flops | bytes accessed | tf_op | source)
XLA Modules:
  0.0 137.4 jit_solution(2591770162382864580)
XLA Ops:
  0.0 135.0 %shard_map.64 = bf16[192,3072]{1,0:T(8,128)(2,1)} custom-call(s32[128]{0:T(128)} %valid_ref.1, bf16[192,3072]{1,0:T(8,128)(2,1)} %q_ref.1, bf16[192,3072]{1,0:T(8,128)(2,1)} %k_ref.1, bf16[192,3072]{1,0:T(8,128)(2,1)} %v_ref.1, s32[1,192]{1,0:T(1,128)} %bitcast.1, s32[4,4]{1,0:T(4,128)} %windows_ref.1), custom_call_target="tpu_custom_call" | custom-call | tf_op jit(solution)/shard_map/pallas_call | solution.py:495
  135.0 2.4 %copy.8 = bf16[192,3072]{1,0:T(8,128)(2,1)} copy(bf16[192,3072]{1,0:T(8,128)(2,1)} %shard_map.64) | data formatting | bytes 2359296
